TPU v7x, 256 devices: a whole 4x4x8 slice. The times are simulated.
256 devices in a mesh: dp: 8 (over x_hi, y), ctx: 32 (over z, x_lo, core).
Axes of the slice: x: 4 (x_hi: 2, x_lo: 2; x = x_hi * 2 + x_lo), y: 4, z: 8, core: 2. Of those that a mesh axis runs over, the one named last changes fastest.
Arguments:
- queries: bfloat16 [65536, 4096], P(('dp', 'ctx')), may hold values from -5 to 5
- conv_keys: bfloat16 [65536, 512], P(('dp', 'ctx')), may hold values from -5 to 5
- conv_values: bfloat16 [65536, 512], P(('dp', 'ctx')), may hold values from -5 to 5
- out_grad: bfloat16 [65536, 4096], P(('dp', 'ctx')), may hold values from -5 to 5
- segment_ids: int32 [256, 256], P(('dp', 'ctx')), may hold values from 0 to 2, never falling along the last dimension, each value on 1 to 128 neighbouring positions
- cart_keys: bfloat16 [1024, 512], P('ctx'), may hold values from -5 to 5
- cart_values: bfloat16 [1024, 512], P('ctx'), may hold values from -5 to 5
Outputs:
- cart_key_grad: float32 [1024, 512], P('ctx')
- cart_value_grad: float32 [1024, 512], P('ctx')
Inputs may be any that keep to these rules, and one draw needn't show every extreme that they name: `segment_ids`: within a block the numbers never fall; each block holds 3 conversations of 1 to 128 tokens, one of exactly 128.
All inputs are finite; a program needn't handle non-finite values.
Results may differ from a plain program's by a relative error of at most 0.0041.
Values may be sent and summed in bfloat16 or wider, within the bound.
No kernel may reach another device: no remote copies, remote signals or barrier semaphores. Data moves between devices by JAX's collectives and lax.ppermute only.
A program may use at most 128 MiB of HBM per device.

v0:
```python
import math

import jax
import jax.numpy as jnp
from jax import lax
from jax.sharding import PartitionSpec as P

HD = 128


def split_heads(array, heads):
    return jnp.moveaxis(array.reshape(array.shape[0], heads, HD), 1, 0)


def group_stats(items, allowed, scale):
    query_group, cart_key, cart_value, conv_key, conv_value = items
    score_cart = (
        jnp.einsum("tgd,jd->tgj", query_group, cart_key, preferred_element_type=jnp.float32) * scale
    )
    score_conv = (
        jnp.einsum("tgd,ud->tgu", query_group, conv_key, preferred_element_type=jnp.float32) * scale
    )
    score_conv = jnp.where(allowed[:, None, :], score_conv, -jnp.inf)
    top = jnp.maximum(jnp.max(score_cart, axis=-1), jnp.max(score_conv, axis=-1))
    exp_cart = jnp.exp(score_cart - top[..., None])
    exp_conv = jnp.exp(score_conv - top[..., None])
    total = jnp.sum(exp_cart, axis=-1) + jnp.sum(exp_conv, axis=-1)
    probs_cart = (exp_cart / total[..., None]).astype(jnp.bfloat16)
    probs_conv = (exp_conv / total[..., None]).astype(jnp.bfloat16)
    mixed = jnp.einsum("tgj,jd->tgd", probs_cart, cart_value, preferred_element_type=jnp.float32)
    mixed = mixed + jnp.einsum(
        "tgu,ud->tgd", probs_conv, conv_value, preferred_element_type=jnp.float32
    )
    return (top, total, mixed)


def group_grads(items, scale):
    query_group, grad_group, top, total, delta, key_rows, value_rows = items
    score = (
        jnp.einsum("tgd,jd->tgj", query_group, key_rows, preferred_element_type=jnp.float32) * scale
    )
    probs = jnp.exp(score - top[..., None]) / total[..., None]
    probs_b = probs.astype(jnp.bfloat16)
    dprob = jnp.einsum("tgd,jd->tgj", grad_group, value_rows, preferred_element_type=jnp.float32)
    dscore_b = (probs * (dprob - delta[..., None])).astype(jnp.bfloat16)
    value_grad = jnp.einsum("tgj,tgd->jd", probs_b, grad_group, preferred_element_type=jnp.float32)
    key_grad = (
        jnp.einsum("tgj,tgd->jd", dscore_b, query_group, preferred_element_type=jnp.float32) * scale
    )
    return (key_grad, value_grad)


def per_device(queries, conv_keys, conv_values, out_grad, segment_ids, cart_keys, cart_values):
    scale = 1.0 / math.sqrt(HD)
    kv_heads = cart_keys.shape[1] // HD
    group = queries.shape[1] // (kv_heads * HD)
    tokens = queries.shape[0]
    full_keys, full_values = (
        lax.all_gather(cart_keys, "ctx", axis=0, tiled=True),
        lax.all_gather(cart_values, "ctx", axis=0, tiled=True),
    )
    segments = segment_ids[0]
    position = jnp.arange(tokens)
    allowed = (segments[:, None] == segments[None, :]) & (position[None, :] <= position[:, None])
    query_heads = jnp.moveaxis(queries.reshape(tokens, kv_heads, group, HD), 1, 0)
    grad_heads = jnp.moveaxis(out_grad.reshape(tokens, kv_heads, group, HD), 1, 0)
    conv_key_heads = split_heads(conv_keys, kv_heads)
    conv_value_heads = split_heads(conv_values, kv_heads)
    tops, totals, mixed = lax.map(
        lambda items: group_stats(items, allowed, scale),
        (
            query_heads,
            split_heads(full_keys, kv_heads),
            split_heads(full_values, kv_heads),
            conv_key_heads,
            conv_value_heads,
        ),
    )
    deltas = jnp.sum(grad_heads.astype(jnp.float32) * mixed, axis=-1)
    count = full_keys.shape[0]
    key_grads, value_grads = lax.map(
        lambda items: group_grads(items, scale),
        (
            query_heads,
            grad_heads,
            tops,
            totals,
            deltas,
            split_heads(full_keys, kv_heads),
            split_heads(full_values, kv_heads),
        ),
    )
    key_part = jnp.moveaxis(key_grads, 0, 1).reshape(count, kv_heads * HD)
    value_part = jnp.moveaxis(value_grads, 0, 1).reshape(count, kv_heads * HD)
    partial_sum = lax.psum_scatter(
        jnp.concatenate([key_part, value_part], axis=1), "ctx", scatter_dimension=0, tiled=True
    )
    summed = lax.psum(partial_sum, "dp")
    return (summed[:, : kv_heads * HD], summed[:, kv_heads * HD :])


def solution(mesh):
    in_specs = (
        P(("dp", "ctx"), None),
        P(("dp", "ctx"), None),
        P(("dp", "ctx"), None),
        P(("dp", "ctx"), None),
        P(("dp", "ctx"), None),
        P("ctx", None),
        P("ctx", None),
    )
    out_specs = (P("ctx", None), P("ctx", None))
    return jax.shard_map(
        per_device, mesh=mesh, in_specs=in_specs, out_specs=out_specs, check_vma=False
    )
```

profile of v0, /device:TPU:32, one launch (start us, length us, event | category | flops | bytes accessed | tf_op | source)
XLA Modules:
  0.0 486.7 jit_solution(3428799468975317941)
XLA Ops:
  8.7 4.1 copy.38
  12.8 3.1 copy.50
  16.9 4.0 copy.48
  21.0 54.2 %all-gather.5.cloned.1.call-done = bf16[1024,512]{1,0:T(8,128)(2,1)} async-done(((bf16[32,512]{1,0:T(8,128)(2,1)}), bf16[1024,512]{1,0:T(8,128)(2,1)}) %all-gather.5.cloned.1.call-update) | async-done | bytes 1048592 | tf_op jit(solution)/shard_map/all_gather | solution.py:60
  78.0 62.4 %all-gather.3.cloned.1.call-done = bf16[1024,512]{1,0:T(8,128)(2,1)} async-done(((bf16[32,512]{1,0:T(8,128)(2,1)}), bf16[1024,512]{1,0:T(8,128)(2,1)}) %all-gather.3.cloned.1.call-update) | async-done | bytes 1048592 | tf_op jit(solution)/shard_map/all_gather | solution.py:59
  143.2 53.2 %while.28 = (s32[]{:T(128)}, f32[4,256,8]{1,2,0:T(8,128)S(1)}, f32[4,256,8]{1,2,0:T(8,128)S(1)}, f32[4,256,8,128]{1,3,2,0:T(8,128)}, bf16[4,256,8,128]{3,1,2,0:T...) while((s32[]{:T(128)}, f32[4,256,8]{1,2,0:T(8,128)S(1)}, ...), condition=%wide.region_5.6_spmd.clone, body=%wide.region_0.5_spmd.clone.sunk | while | flops 1367797760 | bytes 40915572 | solution.py:69
  148.4 2.8 fusion.104
  151.2 2.7 fusion.105
  161.7 2.8 fusion.104
  164.5 2.7 fusion.105
  175.0 2.8 fusion.104
  177.8 2.7 fusion.105
  188.3 2.8 fusion.104
  191.1 2.7 fusion.105
  196.4 3.6 multiply_reduce_fusion.1
  200.0 60.4 %while.27 = (s32[]{:T(128)}, f32[4,1024,128]{2,1,0:T(8,128)}, f32[4,1024,128]{2,1,0:T(8,128)}, bf16[4,256,8,128]{3,1,2,0:T(8,128)(2,1)S(1)}, bf16[4,1024,128]{2,...) while((s32[]{:T(128)}, f32[4,1024,128]{2,1,0:T(8,128)}, ...), condition=%wide.region_8.9_spmd, body=%wide.region_7.8_spmd.sunk | while | flops 2162294784 | bytes 62468240 | solution.py:81
  200.2 2.7 exponential_divide_fusion.2
  203.0 3.6 fusion.97
  206.5 8.8 %fusion.96 = f32[4,1024,128]{2,1,0:T(8,128)} fusion(f32[4,1024,128]{2,1,0:T(8,128)} %get-tuple-element.418, s32[]{:T(128)} %get-tuple-element.417, f32[256,8,1024]{2,0,1:T(8,128)} %copy-done, f32[256,8]{0,1:T(8,128)S(1)} %get-tuple-element.354, bf16[4,256,8,128]{1,3,2,0:T(8,128)(2,1)} %get-tuple-element.435, ...), kind=kOutput, calls=%fused_computation.13.clone.1 | convolution fusion | flops 1080164352 | bytes 10233856 | tf_op jit(solution)/shard_map/while/body/eval_jaxpr/tgj,tgd->jd/dot_general | solution.py:48
  215.3 2.7 exponential_divide_fusion.2
  218.0 3.6 fusion.97
  221.6 8.8 %fusion.96 = f32[4,1024,128]{2,1,0:T(8,128)} fusion(f32[4,1024,128]{2,1,0:T(8,128)} %get-tuple-element.418, s32[]{:T(128)} %get-tuple-element.417, f32[256,8,1024]{2,0,1:T(8,128)} %copy-done, f32[256,8]{0,1:T(8,128)S(1)} %get-tuple-element.354, bf16[4,256,8,128]{1,3,2,0:T(8,128)(2,1)} %get-tuple-element.435, ...), kind=kOutput, calls=%fused_computation.13.clone.1 | convolution fusion | flops 1080164352 | bytes 10233856 | tf_op jit(solution)/shard_map/while/body/eval_jaxpr/tgj,tgd->jd/dot_general | solution.py:48
  230.4 2.7 exponential_divide_fusion.2
  233.1 3.5 fusion.97
  236.6 8.7 %fusion.96 = f32[4,1024,128]{2,1,0:T(8,128)} fusion(f32[4,1024,128]{2,1,0:T(8,128)} %get-tuple-element.418, s32[]{:T(128)} %get-tuple-element.417, f32[256,8,1024]{2,0,1:T(8,128)} %copy-done, f32[256,8]{0,1:T(8,128)S(1)} %get-tuple-element.354, bf16[4,256,8,128]{1,3,2,0:T(8,128)(2,1)} %get-tuple-element.435, ...), kind=kOutput, calls=%fused_computation.13.clone.1 | convolution fusion | flops 1080164352 | bytes 10233856 | tf_op jit(solution)/shard_map/while/body/eval_jaxpr/tgj,tgd->jd/dot_general | solution.py:48
  245.4 2.7 exponential_divide_fusion.2
  248.1 3.5 fusion.97
  251.6 8.7 %fusion.96 = f32[4,1024,128]{2,1,0:T(8,128)} fusion(f32[4,1024,128]{2,1,0:T(8,128)} %get-tuple-element.418, s32[]{:T(128)} %get-tuple-element.417, f32[256,8,1024]{2,0,1:T(8,128)} %copy-done, f32[256,8]{0,1:T(8,128)S(1)} %get-tuple-element.354, bf16[4,256,8,128]{1,3,2,0:T(8,128)(2,1)} %get-tuple-element.435, ...), kind=kOutput, calls=%fused_computation.13.clone.1 | convolution fusion | flops 1080164352 | bytes 10233856 | tf_op jit(solution)/shard_map/while/body/eval_jaxpr/tgj,tgd->jd/dot_general | solution.py:48
  260.4 2.5 copy_bitcast_fusion
  262.9 2.4 pad_maximum_fusion
  265.4 116.2 %reduce-scatter.2.cloned.1.call-done = f32[32,1024]{1,0:T(8,128)} async-done(((f32[1024,1024]{1,0:T(8,128)}), f32[32,1024]{1,0:T(8,128)}) %reduce-scatter.2.cloned.1.call-update) | async-done | bytes 131088 | tf_op jit(solution)/shard_map/reduce_scatter | solution.py:95
  381.6 97.0 %all-reduce.2.cloned.1.call-done = f32[32,1024]{1,0:T(8,128)} async-done(((f32[32,1024]{1,0:T(8,128)}), f32[32,1024]{1,0:T(8,128)}) %all-reduce.2.cloned.1.call-update) | async-done | bytes 131088 | tf_op jit(solution)/shard_map/psum | solution.py:98
  (78 shorter events, 40.9 us)
Async XLA Ops:
  7.2 68.0 %all-gather.5.cloned.1.call-start = ((), (), s32[]{:S(2)}) async-start(), calls=%async_computation.2 | async-start | bytes 1081344 | tf_op jit(solution)/shard_map/all_gather | solution.py:60
  7.9 132.5 %all-gather.3.cloned.1.call-start = ((), (), s32[]{:S(2)}) async-start(), calls=%async_computation.1 | async-start | bytes 1081344 | tf_op jit(solution)/shard_map/all_gather | solution.py:59
  8.6 372.9 %reduce-scatter.2.cloned.1.call-start = ((), (), s32[]{:S(2)}) async-start(), calls=%async_computation.3 | async-start | bytes 4325376 | tf_op jit(solution)/shard_map/reduce_scatter | solution.py:95
  12.8 3.1 copy-start.1
  12.8 3.3 copy-start.2
  78.0 65.2 %copy-start.3 = (s32[1,256]{1,0:T(1,128)S(1)}, s32[1,256]{1,0:T(1,128)}, u32[]{:S(2)}) copy-start(s32[1,256]{1,0:T(1,128)} %param.15) | copy-start | bytes 3076
  202.9 3.6 copy-start
  218.0 3.6 copy-start
  233.1 3.5 copy-start
  248.1 3.5 copy-start
  265.3 213.3 %all-reduce.2.cloned.1.call-start = ((), (), s32[]{:S(2)}) async-start(), calls=%async_computation.4 | async-start | bytes 262144 | tf_op jit(solution)/shard_map/psum | solution.py:98
Sparse Core Ops, SparseCore 0:
  9.9 65.3 all-gather.4
  77.1 63.2 all-gather.2
  265.4 116.0 reduce-scatter.1
  384.1 94.5 all-reduce.1
where the time goes:
time: 488 us; the launch traced here: 487 us
  waiting for transfers between devices  331 us (68%)
  matrix products  93.1 us (19%)
  local copies, waits for them, and re-layouts  32.6 us (7%)
  other arithmetic  15.3 us (3%)
  between operations  13.9 us (3%)
    reduce_scatter x1, waiting for transfers between devices, per_device(): lax.psum_scatter(jnp.concatenate([key_part, value_part], axis=1), 'ctx',...  116 us
    psum x1, waiting for transfers between devices, per_device(): summed = lax.psum(partial_sum, 'dp')  97 us
    all_gather x1, waiting for transfers between devices, per_device(): lax.all_gather(cart_keys, 'ctx', axis=0, tiled=True)  62.4 us
    all_gather x1, waiting for transfers between devices, per_device(): lax.all_gather(cart_values, 'ctx', axis=0, tiled=True)  54.2 us
    dot_general x4, matrix products, group_grads(): jnp.einsum('tgj,tgd->jd', dscore_b, query_group, preferred_element_type=j...  35 us
    dot_general x4, matrix products, group_grads(): jnp.einsum('tgj,tgd->jd', probs_b, grad_group, preferred_element_type=jnp...  14.2 us
    dot_general x4, matrix products, group_stats(): jnp.einsum('tgj,jd->tgd', probs_cart, cart_value, preferred_element_type=...  11.1 us
    dot_general x4, matrix products, group_grads(): jnp.einsum('tgd,jd->tgj', query_group, key_rows, preferred_element_type=j...  10.9 us
  transfers between devices with their start and end apart: 4, of which 4 were waited for; matrix products, arithmetic and copies ran while one was open for 3% of the time, Pallas kernels for 0%

commit v1 on v0

v1 whole, which is shorter than its diff:
```python
import math

import jax
import jax.numpy as jnp
from jax import lax
from jax.experimental import pallas as pl
from jax.experimental.pallas import tpu as pltpu
from jax.sharding import PartitionSpec as P

HD = 128
TOK = 256
CART = 1024
HK = 4
GROUP = 8
HP = 2
CHUNK = 256
SCALE = 1.0 / math.sqrt(HD)
SCALE2 = SCALE * math.log2(math.e)
MASKED = -1e30

f32 = jnp.float32
bf16 = jnp.bfloat16
NT = (((1,), (1,)), ((), ()))
NN = (((1,), (0,)), ((), ()))


def dot(a, b, dims):
    return lax.dot_general(a, b, dims, preferred_element_type=f32)


def head_step(q, g, k_ref, v_ref, conv_k, conv_v, bias, acc):
    rows3 = lambda x: x.reshape(-1, 8, TOK)
    top = total = mixed = None
    held = []
    for c in range(-1, CART // CHUNK):
        if c < 0:
            s = rows3(dot(conv_k, q, NT) * SCALE2 + bias)
            dp = rows3(dot(conv_v, g, NT))
        else:
            rows = pl.ds(c * CHUNK, CHUNK)
            s = rows3(dot(k_ref[rows, :], q, NT) * SCALE2)
            dp = rows3(dot(v_ref[rows, :], g, NT))
        new = jnp.max(s, axis=0)
        if top is not None:
            new = jnp.maximum(top, new)
        e = jnp.exp2(s - new[None])
        part = jnp.sum(e, axis=0)
        mpart = jnp.sum(e * dp, axis=0)
        if top is not None:
            old = jnp.exp2(top - new)
            part = part + total * old
            mpart = mpart + mixed * old
        top, total, mixed = new, part, mpart
        if c >= 0:
            held.append((e, dp, top))
    last = jnp.max(top, axis=0, keepdims=True)
    fix = jnp.exp2(top - last)
    inv = 1.0 / jnp.sum(total * fix, axis=0, keepdims=True)
    delta = jnp.sum(mixed * fix, axis=0, keepdims=True) * inv
    for c, (e, dp, top) in enumerate(held):
        rows = pl.ds(c * CHUNK, CHUNK)
        p = e * (jnp.exp2(top - last) * inv)[None]
        ds = (p * (dp - delta[None])).reshape(CHUNK, TOK).astype(bf16)
        pb = p.reshape(CHUNK, TOK).astype(bf16)
        acc[rows, :HD] += dot(ds, q, NN)
        acc[rows, HD:] += dot(pb, g, NN)


def kernel(seg_row, seg_col, q_ref, g_ref, k_ref, v_ref, ck_ref, cv_ref, own_ref, sent_ref, acc, bias):
    group, step = pl.program_id(0), pl.program_id(1)

    @pl.when(jnp.logical_and(group == 0, step == 0))
    def _():
        key_at = lax.broadcasted_iota(jnp.int32, (TOK, TOK), 0)
        tok_at = lax.broadcasted_iota(jnp.int32, (TOK, TOK), 1)
        ok = (seg_col[...] == seg_row[...]) & (key_at <= tok_at)
        bias[...] = jnp.where(ok, 0.0, MASKED)

    @pl.when(step == 0)
    def _():
        acc[...] = jnp.zeros_like(acc)

    for j in range(HP):
        cols = slice(j * HD, (j + 1) * HD)
        head_step(q_ref[:, cols], g_ref[:, cols], k_ref, v_ref, ck_ref[...], cv_ref[...], bias[...], acc)

    @pl.when(step == GROUP // HP - 1)
    def _():
        half = CART // 2
        own_ref[:, :HD] = acc[:half, :HD] * SCALE
        own_ref[:, HD:] = acc[:half, HD:]
        sent_ref[:, :HD] = (acc[half:, :HD] * SCALE).astype(bf16)
        sent_ref[:, HD:] = acc[half:, HD:].astype(bf16)


def attention(segments, queries, out_grad, rows, conv_keys, conv_values):
    steps = GROUP // HP
    spec = pl.BlockSpec
    return pl.pallas_call(
        kernel,
        grid=(HK, steps),
        in_specs=[
            spec((1, TOK), lambda i, h: (0, 0)),
            spec((TOK, 1), lambda i, h: (0, 0)),
            spec((TOK, HP * HD), lambda i, h: (0, i * steps + h)),
            spec((TOK, HP * HD), lambda i, h: (0, i * steps + h)),
            spec((CART, HD), lambda i, h: (0, i)),
            spec((CART, HD), lambda i, h: (0, HK + i)),
            spec((TOK, HD), lambda i, h: (0, i)),
            spec((TOK, HD), lambda i, h: (0, i)),
        ],
        out_specs=[
            spec((CART // 2, 2 * HD), lambda i, h: (0, i)),
            spec((CART // 2, 2 * HD), lambda i, h: (0, i)),
        ],
        out_shape=[
            jax.ShapeDtypeStruct((CART // 2, 2 * HK * HD), f32),
            jax.ShapeDtypeStruct((CART // 2, 2 * HK * HD), bf16),
        ],
        scratch_shapes=[pltpu.VMEM((CART, 2 * HD), f32), pltpu.VMEM((TOK, TOK), f32)],
        compiler_params=pltpu.CompilerParams(vmem_limit_bytes=48 * 2**20),
    )(segments, segments.reshape(TOK, 1), queries, out_grad, rows, rows, conv_keys, conv_values)


CORE = [(i, i ^ 1) for i in range(32)]
XLO = [(i, i ^ 2) for i in range(32)]


def along_z(k):
    return [(z * 4 + r, ((z + k) % 8) * 4 + r) for z in range(8) for r in range(4)]


def per_device(queries, conv_keys, conv_values, out_grad, segment_ids, cart_keys, cart_values):
    own = jnp.concatenate([cart_keys, cart_values], axis=1)
    rows = jnp.concatenate([own] + [lax.ppermute(own, "ctx", along_z(k)) for k in range(1, 8)], axis=0)
    rows = jnp.concatenate([rows, lax.ppermute(rows, "ctx", XLO)], axis=0)
    rows = jnp.concatenate([rows, lax.ppermute(rows, "ctx", CORE)], axis=0)
    kept, sent = attention(segment_ids, queries, out_grad, rows, conv_keys, conv_values)
    part = kept + lax.ppermute(sent, "ctx", CORE).astype(f32)
    part = part[:256] + lax.ppermute(part[256:].astype(bf16), "ctx", XLO).astype(f32)
    sent = part[32:].astype(bf16)
    total = part[:32]
    for k in range(1, 8):
        total = total + lax.ppermute(sent[(k - 1) * 32 : k * 32], "ctx", along_z(-k)).astype(f32)
    parts = [lax.ppermute(total, "dp", [(i, i ^ k) for i in range(8)]) for k in range(1, 8)]
    level = [total] + parts
    while len(level) > 1:
        level = [level[j] + level[j + 1] for j in range(0, len(level), 2)]
    summed = level[0]
    summed = summed.reshape(32, HK, 2, HD)
    return summed[:, :, 0].reshape(32, HK * HD), summed[:, :, 1].reshape(32, HK * HD)


def solution(mesh):
    every = P(("dp", "ctx"), None)
    return jax.shard_map(
        per_device,
        mesh=mesh,
        in_specs=(every,) * 5 + (P("ctx", None),) * 2,
        out_specs=(P("ctx", None),) * 2,
        check_vma=False,
    )
```

time: 488 us -> 148 us (0.30)
  waiting for transfers between devices: 331 us -> 48.6 us
  matrix products: 93.1 us -> 0 us
  starting transfers between devices: 0.16 us -> 47.2 us
  Pallas kernels: 0 us -> 37.1 us
  local copies, waits for them, and re-layouts: 32.6 us -> 13.2 us
  other arithmetic: 15.3 us -> 0.65 us
  between operations: 13.9 us -> 0.74 us
    all_gather x2 -> x0, waiting for transfers between devices: 117 us -> none  [the longest x1 62.4 us: per_device(): lax.all_gather(cart_keys, 'ctx', axis=0, tiled=True)]
    reduce_scatter x1 -> x0, waiting for transfers between devices: 116 us -> none  [per_device(): lax.psum_scatter(jnp.concatenate([key_part, value_part], axis=1), 'ctx',...]
    psum x1 -> x0, waiting for transfers between devices: 97 us -> none  [per_device(): summed = lax.psum(partial_sum, 'dp')]
    dot_general x28 -> x0, matrix products: 93.1 us -> none  [the longest x4 35 us: group_grads(): jnp.einsum('tgj,tgd->jd', dscore_b, query_group, preferred_element_type=j...]
    ppermute x0 -> x25, waiting for transfers between devices: none -> 48.6 us  [the longest x1 12.5 us: per_device(): lax.ppermute(part[256:].astype(bf16), 'ctx', XLO).astype(f32)]
    ppermute x0 -> x25, starting transfers between devices: none -> 47.2 us  [the longest x7 17.5 us: per_device(): lax.ppermute(own, 'ctx', along_z(k))]
    pallas_call x0 -> x1, Pallas kernels: none -> 37.1 us  [attention(): pl.pallas_call(kernel, grid=(HK, steps), in_specs=[spec((1, TOK), lambda...]
    reduce_sum x9 -> x0, other arithmetic: 12.4 us -> none  [the longest x8 8.88 us: group_stats(): total = jnp.sum(exp_cart, axis=-1) + jnp.sum(exp_conv, axis=-1)]
  transfers between devices with their start and end apart: 4 -> 25, of which waited for: 4 -> 13; matrix products, arithmetic and copies ran while one was open for 3% -> 3% of each run, Pallas kernels for 0% -> 0%
where the time goes in v1:
time: 148 us; the launch traced here: 147 us
  waiting for transfers between devices  48.6 us (33%)
  starting transfers between devices  47.2 us (32%)
  Pallas kernels  37.1 us (25%)
  local copies, waits for them, and re-layouts  13.2 us (9%)
    pallas_call x1, Pallas kernels, attention(): pl.pallas_call(kernel, grid=(HK, steps), in_specs=[spec((1, TOK), lambda...  37.1 us
    ppermute x7, starting transfers between devices, per_device(): lax.ppermute(own, 'ctx', along_z(k))  17.5 us
    ppermute x7, starting transfers between devices, per_device(): lax.ppermute(total, 'dp', [(i, i ^ k) for i in range(8)])  14.9 us
    ppermute x1, waiting for transfers between devices, per_device(): lax.ppermute(part[256:].astype(bf16), 'ctx', XLO).astype(f32)  12.5 us
    ppermute x1, waiting for transfers between devices, per_device(): rows = jnp.concatenate([rows, lax.ppermute(rows, 'ctx', XLO)], axis=0)  12.4 us
    ppermute x7, starting transfers between devices, per_device(): lax.ppermute(sent[(k - 1) * 32:k * 32], 'ctx', along_z(-k)).astype(f32)  11.5 us
    unnamed x19, local copies, waits for them, and re-layouts  8.59 us
    ppermute x7, waiting for transfers between devices, per_device(): lax.ppermute(sent[(k - 1) * 32:k * 32], 'ctx', along_z(-k)).astype(f32)  8.47 us
  transfers between devices with their start and end apart: 25, of which 13 were waited for; matrix products, arithmetic and copies ran while one was open for 3% of the time, Pallas kernels for 0%

profile of v1, /device:TPU:32, one launch (start us, length us, event | category | flops | bytes accessed | tf_op | source)
XLA Modules:
  0.0 147.4 jit_solution(10473181719759834735)
XLA Ops:
  0.6 1.4 constant_dynamic-update-slice_fusion.20
  2.0 1.4 constant_dynamic-update-slice_fusion.19
  3.4 1.9 %collective-permute-start = (bf16[32,1024]{1,0:T(8,128)(2,1)S(1)}, bf16[32,1024]{1,0:T(8,128)(2,1)S(1)}, u32[]{:S(2)}, u32[]{:S(2)}) collective-permute-start(bf16[32,1024]{1,0:T(8,128)(2,1)S(1)} %get-tuple-element.43), channel_id=1, source_target_pairs={{0,4},{1,5},{2,6},{3,7},{4,8},{5,9},{6,10},{7,11},{8,12},{9,13},{1... | collective-permute-start | bytes 196616 | tf_op jit(solution)/shard_map/ppermute | solution.py:135
  5.3 4.5 %collective-permute-start.1 = (bf16[32,1024]{1,0:T(8,128)(2,1)S(1)}, bf16[32,1024]{1,0:T(8,128)(2,1)S(1)}, u32[]{:S(2)}, u32[]{:S(2)}) collective-permute-start(bf16[32,1024]{1,0:T(8,128)(2,1)S(1)} %get-tuple-element.43), channel_id=1, source_target_pairs={{0,8},{1,9},{2,10},{3,11},{4,12},{5,13},{6,14},{7,15},{8,16},{9,17... | collective-permute-start | bytes 196616 | tf_op jit(solution)/shard_map/ppermute | solution.py:135
  9.8 1.9 %collective-permute-start.2 = (bf16[32,1024]{1,0:T(8,128)(2,1)S(1)}, bf16[32,1024]{1,0:T(8,128)(2,1)S(1)}, u32[]{:S(2)}, u32[]{:S(2)}) collective-permute-start(bf16[32,1024]{1,0:T(8,128)(2,1)S(1)} %get-tuple-element.43), channel_id=1, source_target_pairs={{0,12},{1,13},{2,14},{3,15},{4,16},{5,17},{6,18},{7,19},{8,20},{9,... | collective-permute-start | bytes 196616 | tf_op jit(solution)/shard_map/ppermute | solution.py:135
  11.7 1.4 collective-permute-start.3
  13.2 3.0 %collective-permute-start.4 = (bf16[32,1024]{1,0:T(8,128)(2,1)S(1)}, bf16[32,1024]{1,0:T(8,128)(2,1)S(1)}, u32[]{:S(2)}, u32[]{:S(2)}) collective-permute-start(bf16[32,1024]{1,0:T(8,128)(2,1)S(1)} %get-tuple-element.43), channel_id=1, source_target_pairs={{0,20},{1,21},{2,22},{3,23},{4,24},{5,25},{6,26},{7,27},{8,28},{9,... | collective-permute-start | bytes 196616 | tf_op jit(solution)/shard_map/ppermute | solution.py:135
  16.2 2.5 %collective-permute-start.5 = (bf16[32,1024]{1,0:T(8,128)(2,1)S(1)}, bf16[32,1024]{1,0:T(8,128)(2,1)S(1)}, u32[]{:S(2)}, u32[]{:S(2)}) collective-permute-start(bf16[32,1024]{1,0:T(8,128)(2,1)S(1)} %get-tuple-element.43), channel_id=1, source_target_pairs={{0,24},{1,25},{2,26},{3,27},{4,28},{5,29},{6,30},{7,31},{8,0},{9,1... | collective-permute-start | bytes 196616 | tf_op jit(solution)/shard_map/ppermute | solution.py:135
  19.3 2.2 %collective-permute-start.6 = (bf16[32,1024]{1,0:T(8,128)(2,1)S(1)}, bf16[32,1024]{1,0:T(8,128)(2,1)S(1)}, u32[]{:S(2)}, u32[]{:S(2)}) collective-permute-start(bf16[32,1024]{1,0:T(8,128)(2,1)S(1)} %get-tuple-element.43), channel_id=1, source_target_pairs={{0,28},{1,29},{2,30},{3,31},{4,0},{5,1},{6,2},{7,3},{8,4},{9,5},{1... | collective-permute-start | bytes 196616 | tf_op jit(solution)/shard_map/ppermute | solution.py:135
  24.5 2.3 %collective-permute-done.5 = bf16[32,1024]{1,0:T(8,128)(2,1)S(1)} collective-permute-done((bf16[32,1024]{1,0:T(8,128)(2,1)S(1)}, bf16[32,1024]{1,0:T(8,128)(2,1)S(1)}, u32[]{:S(2)}, u32[]{:S(2)}) %collective-permute-start.5) | collective-permute-done | bytes 65568 | tf_op jit(solution)/shard_map/ppermute | solution.py:135
  28.2 1.5 %collective-permute-start.7 = (bf16[256,1024]{1,0:T(8,128)(2,1)S(1)}, bf16[256,1024]{1,0:T(8,128)(2,1)S(1)}, u32[]{:S(2)}, u32[]{:S(2)}) collective-permute-start(bf16[256,1024]{1,0:T(8,128)(2,1)S(1)} %get-tuple-element.21), channel_id=1, source_target_pairs={{0,2},{1,3},{2,0},{3,1},{4,6},{5,7},{6,4},{7,5},{8,10},{9,11},{10,... | collective-permute-start | bytes 1572872 | tf_op jit(solution)/shard_map/ppermute | solution.py:136
  29.7 12.4 %collective-permute-done.7 = bf16[256,1024]{1,0:T(8,128)(2,1)S(1)} collective-permute-done((bf16[256,1024]{1,0:T(8,128)(2,1)S(1)}, bf16[256,1024]{1,0:T(8,128)(2,1)S(1)}, u32[]{:S(2)}, u32[]{:S(2)}) %collective-permute-start.7) | collective-permute-done | bytes 524320 | tf_op jit(solution)/shard_map/ppermute | solution.py:136
  44.5 1.5 %collective-permute-done.8 = bf16[512,1024]{1,0:T(8,128)(2,1)} collective-permute-done((bf16[512,1024]{1,0:T(8,128)(2,1)}, bf16[512,1024]{1,0:T(8,128)(2,1)}, u32[]{:S(2)}, u32[]{:S(2)}) %collective-permute-start.8) | collective-permute-done | bytes 1048608 | tf_op jit(solution)/shard_map/ppermute | solution.py:137
  46.0 2.3 %constant_dynamic-update-slice_fusion.21.k_ref.v_ref = bf16[1024,1024]{1,0:T(8,128)(2,1)} fusion(bf16[1024,1024]{1,0:T(8,128)(2,1)} %copy-done.4, bf16[512,1024]{1,0:T(8,128)(2,1)} %collective-permute-done.8), kind=kLoop, calls=%fused_computation.32 | loop fusion | bytes 2097152 | tf_op jit(solution)/shard_map/concatenate | solution.py:137
  48.3 37.1 %shard_map.86 = (f32[512,1024]{1,0:T(8,128)S(1)}, bf16[512,1024]{1,0:T(8,128)(2,1)S(1)}) custom-call(s32[1,256]{1,0:T(1,128)S(1)} %copy-done.3, s32[256,1]{1,0:T(8,128)S(1)} %copy.9.seg_col, bf16[256,4096]{1,0:T(8,128)(2,1)S(1)} %copy-done, bf16[256,4096]{1,0:T(8,128)(2,1)} %g_ref.1, bf16[1024,1024]{1,0:T(8,128)(2,1)} %constant_dynamic-update-slice_fusion.21.k_ref.v_ref, ...), custom_call_target="tpu_custom_call" | custom-call | tf_op jit(solution)/shard_map/pallas_call | solution.py:99
  85.6 2.5 %collective-permute-done.9 = bf16[512,1024]{1,0:T(8,128)(2,1)S(1)} collective-permute-done((bf16[512,1024]{1,0:T(8,128)(2,1)S(1)}, bf16[512,1024]{1,0:T(8,128)(2,1)S(1)}, u32[]{:S(2)}, u32[]{:S(2)}) %collective-permute-start.9) | collective-permute-done | bytes 1048608 | tf_op jit(solution)/shard_map/ppermute | solution.py:139
  88.5 1.6 %collective-permute-start.10 = (bf16[256,1024]{1,0:T(8,128)(2,1)S(1)}, bf16[256,1024]{1,0:T(8,128)(2,1)S(1)}, u32[]{:S(2)}, u32[]{:S(2)}) collective-permute-start(bf16[256,1024]{1,0:T(8,128)(2,1)S(1)} %slice.87), channel_id=1, source_target_pairs={{0,2},{1,3},{2,0},{3,1},{4,6},{5,7},{6,4},{7,5},{8,10},{9,11},{10,... | collective-permute-start | bytes 1572872 | tf_op jit(solution)/shard_map/ppermute | solution.py:140
  90.1 12.5 %collective-permute-done.10 = bf16[256,1024]{1,0:T(8,128)(2,1)S(1)} collective-permute-done((bf16[256,1024]{1,0:T(8,128)(2,1)S(1)}, bf16[256,1024]{1,0:T(8,128)(2,1)S(1)}, u32[]{:S(2)}, u32[]{:S(2)}) %collective-permute-start.10) | collective-permute-done | bytes 524320 | tf_op jit(solution)/shard_map/ppermute | solution.py:140
  102.9 1.8 %collective-permute-start.12 = (bf16[32,1024]{1,0:T(8,128)(2,1)S(1)}, bf16[32,1024]{1,0:T(8,128)(2,1)S(1)}, u32[]{:S(2)}, u32[]{:S(2)}) collective-permute-start(bf16[32,1024]{1,0:T(8,128)(2,1)S(1)} %get-tuple-element.16), channel_id=1, source_target_pairs={{0,24},{1,25},{2,26},{3,27},{4,28},{5,29},{6,30},{7,31},{8,0},{9,1... | collective-permute-start | bytes 196616 | tf_op jit(solution)/shard_map/ppermute | solution.py:144
  104.8 3.0 %collective-permute-start.13 = (bf16[32,1024]{1,0:T(8,128)(2,1)S(1)}, bf16[32,1024]{1,0:T(8,128)(2,1)S(1)}, u32[]{:S(2)}, u32[]{:S(2)}) collective-permute-start(bf16[32,1024]{1,0:T(8,128)(2,1)S(1)} %get-tuple-element.15), channel_id=1, source_target_pairs={{0,20},{1,21},{2,22},{3,23},{4,24},{5,25},{6,26},{7,27},{8,28},{9,... | collective-permute-start | bytes 196616 | tf_op jit(solution)/shard_map/ppermute | solution.py:144
  107.8 3.0 %collective-permute-start.14 = (bf16[32,1024]{1,0:T(8,128)(2,1)S(1)}, bf16[32,1024]{1,0:T(8,128)(2,1)S(1)}, u32[]{:S(2)}, u32[]{:S(2)}) collective-permute-start(bf16[32,1024]{1,0:T(8,128)(2,1)S(1)} %get-tuple-element.14), channel_id=1, source_target_pairs={{0,16},{1,17},{2,18},{3,19},{4,20},{5,21},{6,22},{7,23},{8,24},{9,... | collective-permute-start | bytes 196616 | tf_op jit(solution)/shard_map/ppermute | solution.py:144
  110.8 1.7 %collective-permute-start.15 = (bf16[32,1024]{1,0:T(8,128)(2,1)S(1)}, bf16[32,1024]{1,0:T(8,128)(2,1)S(1)}, u32[]{:S(2)}, u32[]{:S(2)}) collective-permute-start(bf16[32,1024]{1,0:T(8,128)(2,1)S(1)} %get-tuple-element.13), channel_id=1, source_target_pairs={{0,12},{1,13},{2,14},{3,15},{4,16},{5,17},{6,18},{7,19},{8,20},{9,... | collective-permute-start | bytes 196616 | tf_op jit(solution)/shard_map/ppermute | solution.py:144
  114.4 3.8 %collective-permute-done.13 = bf16[32,1024]{1,0:T(8,128)(2,1)S(1)} collective-permute-done((bf16[32,1024]{1,0:T(8,128)(2,1)S(1)}, bf16[32,1024]{1,0:T(8,128)(2,1)S(1)}, u32[]{:S(2)}, u32[]{:S(2)}) %collective-permute-start.13) | collective-permute-done | bytes 65568 | tf_op jit(solution)/shard_map/ppermute | solution.py:144
  118.2 2.6 %collective-permute-done.15 = bf16[32,1024]{1,0:T(8,128)(2,1)S(1)} collective-permute-done((bf16[32,1024]{1,0:T(8,128)(2,1)S(1)}, bf16[32,1024]{1,0:T(8,128)(2,1)S(1)}, u32[]{:S(2)}, u32[]{:S(2)}) %collective-permute-start.15) | collective-permute-done | bytes 65568 | tf_op jit(solution)/shard_map/ppermute | solution.py:144
  120.7 2.1 %collective-permute-done.16 = bf16[32,1024]{1,0:T(8,128)(2,1)S(1)} collective-permute-done((bf16[32,1024]{1,0:T(8,128)(2,1)S(1)}, bf16[32,1024]{1,0:T(8,128)(2,1)S(1)}, u32[]{:S(2)}, u32[]{:S(2)}) %collective-permute-start.16) | collective-permute-done | bytes 65568 | tf_op jit(solution)/shard_map/ppermute | solution.py:144
  122.9 1.7 %collective-permute-start.18 = (f32[32,1024]{1,0:T(8,128)S(1)}, f32[32,1024]{1,0:T(8,128)S(1)}, u32[]{:S(2)}, u32[]{:S(2)}) collective-permute-start(f32[32,1024]{1,0:T(8,128)S(1)} %fusion.5), channel_id=1, source_target_pairs={{0,32},{32,0},{64,96},{96,64},{128,160},{160,128},{192,224},{224,1... | collective-permute-start | bytes 393224 | tf_op jit(solution)/shard_map/ppermute | solution.py:145
  124.6 2.9 %collective-permute-start.19 = (f32[32,1024]{1,0:T(8,128)S(1)}, f32[32,1024]{1,0:T(8,128)S(1)}, u32[]{:S(2)}, u32[]{:S(2)}) collective-permute-start(f32[32,1024]{1,0:T(8,128)S(1)} %fusion.5), channel_id=1, source_target_pairs={{0,64},{32,96},{64,0},{96,32},{128,192},{160,224},{192,128},{224,1... | collective-permute-start | bytes 393224 | tf_op jit(solution)/shard_map/ppermute | solution.py:145
  127.7 3.0 %collective-permute-start.21 = (f32[32,1024]{1,0:T(8,128)S(1)}, f32[32,1024]{1,0:T(8,128)S(1)}, u32[]{:S(2)}, u32[]{:S(2)}) collective-permute-start(f32[32,1024]{1,0:T(8,128)S(1)} %fusion.5), channel_id=1, source_target_pairs={{0,128},{32,160},{64,192},{96,224},{128,0},{160,32},{192,64},{224,... | collective-permute-start | bytes 393224 | tf_op jit(solution)/shard_map/ppermute | solution.py:145
  131.1 6.6 %collective-permute-start.23 = (f32[32,1024]{1,0:T(8,128)S(1)}, f32[32,1024]{1,0:T(8,128)S(1)}, u32[]{:S(2)}, u32[]{:S(2)}) collective-permute-start(f32[32,1024]{1,0:T(8,128)S(1)} %fusion.5), channel_id=1, source_target_pairs={{0,192},{32,224},{64,128},{96,160},{128,64},{160,96},{192,0},{224,... | collective-permute-start | bytes 393224 | tf_op jit(solution)/shard_map/ppermute | solution.py:145
  137.8 1.8 %collective-permute-done.22 = f32[32,1024]{1,0:T(8,128)S(1)} collective-permute-done((f32[32,1024]{1,0:T(8,128)S(1)}, f32[32,1024]{1,0:T(8,128)S(1)}, u32[]{:S(2)}, u32[]{:S(2)}) %collective-permute-start.22) | collective-permute-done | bytes 131104 | tf_op jit(solution)/shard_map/ppermute | solution.py:145
  139.6 4.1 %collective-permute-done.23 = f32[32,1024]{1,0:T(8,128)S(1)} collective-permute-done((f32[32,1024]{1,0:T(8,128)S(1)}, f32[32,1024]{1,0:T(8,128)S(1)}, u32[]{:S(2)}, u32[]{:S(2)}) %collective-permute-start.23) | collective-permute-done | bytes 131104 | tf_op jit(solution)/shard_map/ppermute | solution.py:145
  143.7 2.6 %collective-permute-done.24 = f32[32,1024]{1,0:T(8,128)S(1)} collective-permute-done((f32[32,1024]{1,0:T(8,128)S(1)}, f32[32,1024]{1,0:T(8,128)S(1)}, u32[]{:S(2)}, u32[]{:S(2)}) %collective-permute-start.24) | collective-permute-done | bytes 131104 | tf_op jit(solution)/shard_map/ppermute | solution.py:145
  (50 shorter events, 12.2 us)
Async XLA Ops:
  0.6 43.7 %copy-start.3 = (s32[1,256]{1,0:T(1,128)S(1)}, s32[1,256]{1,0:T(1,128)}, u32[]{:S(2)}) copy-start(s32[1,256]{1,0:T(1,128)} %seg_row.1) | copy-start | bytes 3076
  3.4 12.8 %collective-permute-start = (bf16[32,1024]{1,0:T(8,128)(2,1)S(1)}, bf16[32,1024]{1,0:T(8,128)(2,1)S(1)}, u32[]{:S(2)}, u32[]{:S(2)}) collective-permute-start(bf16[32,1024]{1,0:T(8,128)(2,1)S(1)} %get-tuple-element.43), channel_id=1, source_target_pairs={{0,4},{1,5},{2,6},{3,7},{4,8},{5,9},{6,10},{7,11},{8,12},{9,13},{1... | collective-permute-start | bytes 196616 | tf_op jit(solution)/shard_map/ppermute | solution.py:135
  5.3 14.0 %collective-permute-start.1 = (bf16[32,1024]{1,0:T(8,128)(2,1)S(1)}, bf16[32,1024]{1,0:T(8,128)(2,1)S(1)}, u32[]{:S(2)}, u32[]{:S(2)}) collective-permute-start(bf16[32,1024]{1,0:T(8,128)(2,1)S(1)} %get-tuple-element.43), channel_id=1, source_target_pairs={{0,8},{1,9},{2,10},{3,11},{4,12},{5,13},{6,14},{7,15},{8,16},{9,17... | collective-permute-start | bytes 196616 | tf_op jit(solution)/shard_map/ppermute | solution.py:135
  9.8 12.4 %collective-permute-start.2 = (bf16[32,1024]{1,0:T(8,128)(2,1)S(1)}, bf16[32,1024]{1,0:T(8,128)(2,1)S(1)}, u32[]{:S(2)}, u32[]{:S(2)}) collective-permute-start(bf16[32,1024]{1,0:T(8,128)(2,1)S(1)} %get-tuple-element.43), channel_id=1, source_target_pairs={{0,12},{1,13},{2,14},{3,15},{4,16},{5,17},{6,18},{7,19},{8,20},{9,... | collective-permute-start | bytes 196616 | tf_op jit(solution)/shard_map/ppermute | solution.py:135
  11.7 11.1 %collective-permute-start.3 = (bf16[32,1024]{1,0:T(8,128)(2,1)S(1)}, bf16[32,1024]{1,0:T(8,128)(2,1)S(1)}, u32[]{:S(2)}, u32[]{:S(2)}) collective-permute-start(bf16[32,1024]{1,0:T(8,128)(2,1)S(1)} %get-tuple-element.43), channel_id=1, source_target_pairs={{0,16},{1,17},{2,18},{3,19},{4,20},{5,21},{6,22},{7,23},{8,24},{9,... | collective-permute-start | bytes 196616 | tf_op jit(solution)/shard_map/ppermute | solution.py:135
  13.2 10.7 %collective-permute-start.4 = (bf16[32,1024]{1,0:T(8,128)(2,1)S(1)}, bf16[32,1024]{1,0:T(8,128)(2,1)S(1)}, u32[]{:S(2)}, u32[]{:S(2)}) collective-permute-start(bf16[32,1024]{1,0:T(8,128)(2,1)S(1)} %get-tuple-element.43), channel_id=1, source_target_pairs={{0,20},{1,21},{2,22},{3,23},{4,24},{5,25},{6,26},{7,27},{8,28},{9,... | collective-permute-start | bytes 196616 | tf_op jit(solution)/shard_map/ppermute | solution.py:135
  16.2 10.5 %collective-permute-start.5 = (bf16[32,1024]{1,0:T(8,128)(2,1)S(1)}, bf16[32,1024]{1,0:T(8,128)(2,1)S(1)}, u32[]{:S(2)}, u32[]{:S(2)}) collective-permute-start(bf16[32,1024]{1,0:T(8,128)(2,1)S(1)} %get-tuple-element.43), channel_id=1, source_target_pairs={{0,24},{1,25},{2,26},{3,27},{4,28},{5,29},{6,30},{7,31},{8,0},{9,1... | collective-permute-start | bytes 196616 | tf_op jit(solution)/shard_map/ppermute | solution.py:135
  19.3 8.2 %collective-permute-start.6 = (bf16[32,1024]{1,0:T(8,128)(2,1)S(1)}, bf16[32,1024]{1,0:T(8,128)(2,1)S(1)}, u32[]{:S(2)}, u32[]{:S(2)}) collective-permute-start(bf16[32,1024]{1,0:T(8,128)(2,1)S(1)} %get-tuple-element.43), channel_id=1, source_target_pairs={{0,28},{1,29},{2,30},{3,31},{4,0},{5,1},{6,2},{7,3},{8,4},{9,5},{1... | collective-permute-start | bytes 196616 | tf_op jit(solution)/shard_map/ppermute | solution.py:135
  27.4 20.9 %copy-start = (bf16[256,4096]{1,0:T(8,128)(2,1)S(1)}, bf16[256,4096]{1,0:T(8,128)(2,1)}, u32[]{:S(2)}) copy-start(bf16[256,4096]{1,0:T(8,128)(2,1)} %q_ref.1) | copy-start | bytes 6291460
  27.4 20.9 %copy-start.1 = (bf16[256,512]{1,0:T(8,128)(2,1)S(1)}, bf16[256,512]{1,0:T(8,128)(2,1)}, u32[]{:S(2)}) copy-start(bf16[256,512]{1,0:T(8,128)(2,1)} %ck_ref.1) | copy-start | bytes 786436
  27.4 20.9 %copy-start.2 = (bf16[256,512]{1,0:T(8,128)(2,1)S(1)}, bf16[256,512]{1,0:T(8,128)(2,1)}, u32[]{:S(2)}) copy-start(bf16[256,512]{1,0:T(8,128)(2,1)} %cv_ref.1) | copy-start | bytes 786436
  28.2 13.8 %collective-permute-start.7 = (bf16[256,1024]{1,0:T(8,128)(2,1)S(1)}, bf16[256,1024]{1,0:T(8,128)(2,1)S(1)}, u32[]{:S(2)}, u32[]{:S(2)}) collective-permute-start(bf16[256,1024]{1,0:T(8,128)(2,1)S(1)} %get-tuple-element.21), channel_id=1, source_target_pairs={{0,2},{1,3},{2,0},{3,1},{4,6},{5,7},{6,4},{7,5},{8,10},{9,11},{10,... | collective-permute-start | bytes 1572872 | tf_op jit(solution)/shard_map/ppermute | solution.py:136
  43.0 1.4 copy-start.4
  43.0 3.0 %collective-permute-start.8 = (bf16[512,1024]{1,0:T(8,128)(2,1)}, bf16[512,1024]{1,0:T(8,128)(2,1)}, u32[]{:S(2)}, u32[]{:S(2)}) collective-permute-start(bf16[512,1024]{1,0:T(8,128)(2,1)} %get-tuple-element.17), channel_id=1, source_target_pairs={{0,1},{1,0},{2,3},{3,2},{4,5},{5,4},{6,7},{7,6},{8,9},{9,8},{10,11... | collective-permute-start | bytes 3145736 | tf_op jit(solution)/shard_map/ppermute | solution.py:137
  85.4 2.7 %collective-permute-start.9 = (bf16[512,1024]{1,0:T(8,128)(2,1)S(1)}, bf16[512,1024]{1,0:T(8,128)(2,1)S(1)}, u32[]{:S(2)}, u32[]{:S(2)}) collective-permute-start(bf16[512,1024]{1,0:T(8,128)(2,1)S(1)} %get-tuple-element.5), channel_id=1, source_target_pairs={{0,1},{1,0},{2,3},{3,2},{4,5},{5,4},{6,7},{7,6},{8,9},{9,8},{10,11... | collective-permute-start | bytes 3145736 | tf_op jit(solution)/shard_map/ppermute | solution.py:139
  88.5 14.1 %collective-permute-start.10 = (bf16[256,1024]{1,0:T(8,128)(2,1)S(1)}, bf16[256,1024]{1,0:T(8,128)(2,1)S(1)}, u32[]{:S(2)}, u32[]{:S(2)}) collective-permute-start(bf16[256,1024]{1,0:T(8,128)(2,1)S(1)} %slice.87), channel_id=1, source_target_pairs={{0,2},{1,3},{2,0},{3,1},{4,6},{5,7},{6,4},{7,5},{8,10},{9,11},{10,... | collective-permute-start | bytes 1572872 | tf_op jit(solution)/shard_map/ppermute | solution.py:140
  102.8 9.7 %collective-permute-start.11 = (bf16[32,1024]{1,0:T(8,128)(2,1)S(1)}, bf16[32,1024]{1,0:T(8,128)(2,1)S(1)}, u32[]{:S(2)}, u32[]{:S(2)}) collective-permute-start(bf16[32,1024]{1,0:T(8,128)(2,1)S(1)} %get-tuple-element.10), channel_id=1, source_target_pairs={{0,28},{1,29},{2,30},{3,31},{4,0},{5,1},{6,2},{7,3},{8,4},{9,5},{1... | collective-permute-start | bytes 196616 | tf_op jit(solution)/shard_map/ppermute | solution.py:144
  102.9 10.6 %collective-permute-start.12 = (bf16[32,1024]{1,0:T(8,128)(2,1)S(1)}, bf16[32,1024]{1,0:T(8,128)(2,1)S(1)}, u32[]{:S(2)}, u32[]{:S(2)}) collective-permute-start(bf16[32,1024]{1,0:T(8,128)(2,1)S(1)} %get-tuple-element.16), channel_id=1, source_target_pairs={{0,24},{1,25},{2,26},{3,27},{4,28},{5,29},{6,30},{7,31},{8,0},{9,1... | collective-permute-start | bytes 196616 | tf_op jit(solution)/shard_map/ppermute | solution.py:144
  104.8 13.4 %collective-permute-start.13 = (bf16[32,1024]{1,0:T(8,128)(2,1)S(1)}, bf16[32,1024]{1,0:T(8,128)(2,1)S(1)}, u32[]{:S(2)}, u32[]{:S(2)}) collective-permute-start(bf16[32,1024]{1,0:T(8,128)(2,1)S(1)} %get-tuple-element.15), channel_id=1, source_target_pairs={{0,20},{1,21},{2,22},{3,23},{4,24},{5,25},{6,26},{7,27},{8,28},{9,... | collective-permute-start | bytes 196616 | tf_op jit(solution)/shard_map/ppermute | solution.py:144
  107.8 10.4 %collective-permute-start.14 = (bf16[32,1024]{1,0:T(8,128)(2,1)S(1)}, bf16[32,1024]{1,0:T(8,128)(2,1)S(1)}, u32[]{:S(2)}, u32[]{:S(2)}) collective-permute-start(bf16[32,1024]{1,0:T(8,128)(2,1)S(1)} %get-tuple-element.14), channel_id=1, source_target_pairs={{0,16},{1,17},{2,18},{3,19},{4,20},{5,21},{6,22},{7,23},{8,24},{9,... | collective-permute-start | bytes 196616 | tf_op jit(solution)/shard_map/ppermute | solution.py:144
  110.8 9.9 %collective-permute-start.15 = (bf16[32,1024]{1,0:T(8,128)(2,1)S(1)}, bf16[32,1024]{1,0:T(8,128)(2,1)S(1)}, u32[]{:S(2)}, u32[]{:S(2)}) collective-permute-start(bf16[32,1024]{1,0:T(8,128)(2,1)S(1)} %get-tuple-element.13), channel_id=1, source_target_pairs={{0,12},{1,13},{2,14},{3,15},{4,16},{5,17},{6,18},{7,19},{8,20},{9,... | collective-permute-start | bytes 196616 | tf_op jit(solution)/shard_map/ppermute | solution.py:144
  112.5 10.3 %collective-permute-start.16 = (bf16[32,1024]{1,0:T(8,128)(2,1)S(1)}, bf16[32,1024]{1,0:T(8,128)(2,1)S(1)}, u32[]{:S(2)}, u32[]{:S(2)}) collective-permute-start(bf16[32,1024]{1,0:T(8,128)(2,1)S(1)} %get-tuple-element.12), channel_id=1, source_target_pairs={{0,8},{1,9},{2,10},{3,11},{4,12},{5,13},{6,14},{7,15},{8,16},{9,17... | collective-permute-start | bytes 196616 | tf_op jit(solution)/shard_map/ppermute | solution.py:144
  113.5 9.4 %collective-permute-start.17 = (bf16[32,1024]{1,0:T(8,128)(2,1)S(1)}, bf16[32,1024]{1,0:T(8,128)(2,1)S(1)}, u32[]{:S(2)}, u32[]{:S(2)}) collective-permute-start(bf16[32,1024]{1,0:T(8,128)(2,1)S(1)} %get-tuple-element.11), channel_id=1, source_target_pairs={{0,4},{1,5},{2,6},{3,7},{4,8},{5,9},{6,10},{7,11},{8,12},{9,13},{1... | collective-permute-start | bytes 196616 | tf_op jit(solution)/shard_map/ppermute | solution.py:144
  122.9 8.1 %collective-permute-start.18 = (f32[32,1024]{1,0:T(8,128)S(1)}, f32[32,1024]{1,0:T(8,128)S(1)}, u32[]{:S(2)}, u32[]{:S(2)}) collective-permute-start(f32[32,1024]{1,0:T(8,128)S(1)} %fusion.5), channel_id=1, source_target_pairs={{0,32},{32,0},{64,96},{96,64},{128,160},{160,128},{192,224},{224,1... | collective-permute-start | bytes 393224 | tf_op jit(solution)/shard_map/ppermute | solution.py:145
  124.6 13.0 %collective-permute-start.19 = (f32[32,1024]{1,0:T(8,128)S(1)}, f32[32,1024]{1,0:T(8,128)S(1)}, u32[]{:S(2)}, u32[]{:S(2)}) collective-permute-start(f32[32,1024]{1,0:T(8,128)S(1)} %fusion.5), channel_id=1, source_target_pairs={{0,64},{32,96},{64,0},{96,32},{128,192},{160,224},{192,128},{224,1... | collective-permute-start | bytes 393224 | tf_op jit(solution)/shard_map/ppermute | solution.py:145
  127.5 10.3 %collective-permute-start.20 = (f32[32,1024]{1,0:T(8,128)S(1)}, f32[32,1024]{1,0:T(8,128)S(1)}, u32[]{:S(2)}, u32[]{:S(2)}) collective-permute-start(f32[32,1024]{1,0:T(8,128)S(1)} %fusion.5), channel_id=1, source_target_pairs={{0,96},{32,64},{64,32},{96,0},{128,224},{160,192},{192,160},{224,1... | collective-permute-start | bytes 393224 | tf_op jit(solution)/shard_map/ppermute | solution.py:145
  127.7 10.1 %collective-permute-start.21 = (f32[32,1024]{1,0:T(8,128)S(1)}, f32[32,1024]{1,0:T(8,128)S(1)}, u32[]{:S(2)}, u32[]{:S(2)}) collective-permute-start(f32[32,1024]{1,0:T(8,128)S(1)} %fusion.5), channel_id=1, source_target_pairs={{0,128},{32,160},{64,192},{96,224},{128,0},{160,32},{192,64},{224,... | collective-permute-start | bytes 393224 | tf_op jit(solution)/shard_map/ppermute | solution.py:145
  130.7 8.8 %collective-permute-start.22 = (f32[32,1024]{1,0:T(8,128)S(1)}, f32[32,1024]{1,0:T(8,128)S(1)}, u32[]{:S(2)}, u32[]{:S(2)}) collective-permute-start(f32[32,1024]{1,0:T(8,128)S(1)} %fusion.5), channel_id=1, source_target_pairs={{0,160},{32,128},{64,224},{96,192},{128,32},{160,0},{192,96},{224,... | collective-permute-start | bytes 393224 | tf_op jit(solution)/shard_map/ppermute | solution.py:145
  131.1 12.6 %collective-permute-start.23 = (f32[32,1024]{1,0:T(8,128)S(1)}, f32[32,1024]{1,0:T(8,128)S(1)}, u32[]{:S(2)}, u32[]{:S(2)}) collective-permute-start(f32[32,1024]{1,0:T(8,128)S(1)} %fusion.5), channel_id=1, source_target_pairs={{0,192},{32,224},{64,128},{96,160},{128,64},{160,96},{192,0},{224,... | collective-permute-start | bytes 393224 | tf_op jit(solution)/shard_map/ppermute | solution.py:145
  137.6 8.6 %collective-permute-start.24 = (f32[32,1024]{1,0:T(8,128)S(1)}, f32[32,1024]{1,0:T(8,128)S(1)}, u32[]{:S(2)}, u32[]{:S(2)}) collective-permute-start(f32[32,1024]{1,0:T(8,128)S(1)} %fusion.5), channel_id=1, source_target_pairs={{0,224},{32,192},{64,160},{96,128},{128,96},{160,64},{192,32},{224... | collective-permute-start | bytes 393224 | tf_op jit(solution)/shard_map/ppermute | solution.py:145
